TPU v7x, 128 devices: a whole 4x4x4 slice. The times are simulated.
128 devices in a mesh: row: 8 (over x, core), col: 16 (over z, y).
Axes of the slice: x: 4, y: 4, z: 4, core: 2. Of those that a mesh axis runs over, the one named last changes fastest.
Arguments:
- right_side: float32 [1024, 2, 256], P(('row', 'col')), may hold values from -12 to 12
- anchor: float32 [1024, 256], P(('row', 'col')), may hold values from 0.3 to 3
- tiles: float32 [1024, 4, 256, 256], P(('row', 'col')), may hold values from 0 to 1, as said below
- neighbours: int32 [1024, 4], P(('row', 'col')), may hold values from 0 to 1023, as said below
- owners: int32 [262144, 1], P(('row', 'col')), may hold values from 0 to 127; in each aligned block of 2048 rows (0 to 2047, 2048 to 4095, ...) at most 32 rows name the same one
- row_offset: int32 [262144], P(('row', 'col')), may hold values from 0 to 2047
- col_offset: int32 [262144], P(('row', 'col')), may hold values from 0 to 511
- macro_density: float32 [16384, 8192], P('row', 'col'), may hold values from 0.05 to 1
Outputs:
- solution: float32 [1024, 2, 256], P(('row', 'col'))
- density: float32 [16384, 8192], P('row', 'col')
Inputs may be any that keep to these rules, and one draw needn't show every extreme that they name: `owners`: at most 32 of the clusters of one device name the same owner; in every draw the clusters of some device name one owner exactly 32 times. `neighbours`: block b lies on device b // 8, and device d on mesh position (d // 16, d % 16) of row and col. Every tile names a block on the device of its own block row or on a device next to it along row, col or both (diagonals included). `tiles`: entries are positive.
All inputs are finite; a program needn't handle non-finite values.
Results may differ from a plain program's by a relative error of at most 0.0003.
Values sent between devices are 32-bit elements; how exact they have to be, the bound alone decides.
A program may use at most 128 MiB of HBM per device.

v0:
```python
import jax
import jax.numpy as jnp
from jax import lax
from jax.sharding import PartitionSpec as P

ITERS = 3
STEPS = 4
HIGH = lax.Precision.HIGHEST
RATE = 0.2


def passed_along(block, axis, distance):
    devices = range(lax.axis_size(axis))
    route = [(i - distance, i) for i in devices if i - distance in devices]
    return lax.ppermute(block, axis, route)


def extended(value, sides, width):
    for axis, dim in sides:
        size, length = (lax.axis_size(axis), value.shape[dim])
        up = [(i, (i + 1) % size) for i in range(size - 1)]
        down = [(j, i) for i, j in up]
        last = lax.slice_in_dim(value, length - width, length, axis=dim)
        leading = lax.slice_in_dim(value, 0, width, axis=dim)
        before = lax.ppermute(last, axis, up)
        after = lax.ppermute(leading, axis, down)
        value = jnp.concatenate([before, value, after], axis=dim)
    return value


def tile_terms(tiles, row_sums, col_sums, own_dir, remote):
    direct = jnp.einsum("bkij,bkcj->bci", tiles, remote, precision=HIGH)
    backward = jnp.einsum("bkij,bci->bkcj", tiles, own_dir, precision=HIGH)
    row_part = row_sums[:, None, :] * own_dir - direct
    col_part = col_sums[:, :, None, :] * remote - backward
    return (row_part, col_part)


def diffuse(padded):
    centre = padded[1:-1, 1:-1]
    return centre + RATE * (
        padded[2:, 1:-1] + padded[:-2, 1:-1] + padded[1:-1, 2:] + padded[1:-1, :-2] - 4.0 * centre
    )


def run_solver(image_of, curve_of, norm_of, start_rhs):
    solution = jnp.zeros_like(start_rhs)
    residual = start_rhs
    direction = start_rhs
    norm_now = norm_of(residual)
    for sweep in range(ITERS):
        image = image_of(direction)
        alpha = norm_now / curve_of(direction, image)
        solution = solution + alpha[None, :, None] * direction
        residual = residual - alpha[None, :, None] * image
        norm_next = norm_of(residual)
        direction = residual + (norm_next / norm_now)[None, :, None] * direction
        norm_now = norm_next
    return solution


def send_col(terms, offset):
    return passed_along(terms, "col", offset)


def send_row(terms, offset):
    return passed_along(terms, "row", offset)


def per_device(
    right_side, anchor, tiles, neighbours, owners, row_offset, col_offset, macro_density
):
    blocks_own = tiles.shape[0]
    fanout = tiles.shape[1]
    width_tile = tiles.shape[2]
    row_sums = jnp.sum(jnp.sum(tiles, axis=3), axis=1)
    col_sums = jnp.sum(tiles, axis=2)
    flat_nbr = neighbours.reshape(-1)
    rows_mesh = lax.axis_size("row")
    cols_mesh = lax.axis_size("col")
    devices_all = rows_mesh * cols_mesh
    device_me = lax.axis_index(("row", "col"))
    mesh_row = device_me // cols_mesh
    mesh_col = device_me % cols_mesh
    named_dev = flat_nbr // blocks_own
    near_slot = (
        (named_dev // cols_mesh - mesh_row + 1) * 3 + (named_dev % cols_mesh - mesh_col + 1)
    ) * blocks_own + flat_nbr % blocks_own
    slot_select = (near_slot[None, :] == lax.iota(jnp.int32, 9 * blocks_own)[:, None]).astype(
        jnp.float32
    )

    def image_of(direction):
        padded = extended(direction[None, None], (("row", 0), ("col", 1)), 1)
        near_blocks = padded.reshape(9 * blocks_own, 2, width_tile)
        remote = near_blocks[near_slot].reshape(blocks_own, fanout, 2, width_tile)
        row_part, col_part = tile_terms(tiles, row_sums, col_sums, direction, remote)
        flat_terms = col_part.reshape(blocks_own * fanout, 2 * width_tile)
        back = jnp.dot(slot_select, flat_terms, precision=HIGH).reshape(
            3, 3, blocks_own, 2, width_tile
        )
        merged_col = back[:, 1] + send_col(back[:, 0], -1) + send_col(back[:, 2], 1)
        incoming = merged_col[1] + send_row(merged_col[0], -1) + send_row(merged_col[2], 1)
        return anchor[:, None, :] * direction + row_part + incoming

    def curve_of(direction, image):
        return lax.psum(jnp.sum(direction * image, axis=(0, 2)), ("row", "col"))

    def norm_of(resid):
        return lax.psum(jnp.sum(resid * resid, axis=(0, 2)), ("row", "col"))

    solution = run_solver(image_of, curve_of, norm_of, right_side)
    clusters_own = blocks_own * width_tile
    by_coord = solution.transpose(1, 0, 2).reshape(2, clusters_own)
    pos_row = row_offset.astype(jnp.float32) + 3.0 * jnp.tanh(by_coord[0])
    pos_col = col_offset.astype(jnp.float32) + 3.0 * jnp.tanh(by_coord[1])
    capacity = max(2, 2 * clusters_own // devices_all)
    target = owners[:, 0]
    matches = (target[:, None] == lax.iota(jnp.int32, devices_all)[None, :]).astype(jnp.int32)
    before = jnp.cumsum(matches, axis=0) - matches
    rank_in = jnp.sum(before * matches, axis=1)
    slot_index = target * capacity + rank_in
    outgoing = jnp.full((2, devices_all * capacity), -1000.0, jnp.float32)
    outgoing = outgoing.at[:, slot_index].set(jnp.stack([pos_row, pos_col]))
    arrived = lax.all_to_all(
        outgoing.reshape(2, devices_all, capacity),
        ("row", "col"),
        split_axis=1,
        concat_axis=1,
        tiled=True,
    )
    arrived = arrived.reshape(2, devices_all * capacity)
    grid_rows = macro_density.shape[0]
    grid_cols = macro_density.shape[1]

    def window_of(position, limit):
        start_cell = jnp.clip(jnp.floor(position).astype(jnp.int32) - 7, 0, limit - 16)
        cells = lax.iota(jnp.int32, limit)[None, :]
        inside = ((cells >= start_cell[:, None]) & (cells < start_cell[:, None] + 16)).astype(
            jnp.float32
        )
        offset = cells.astype(jnp.float32) - position[:, None]
        return (jnp.exp(-0.5 * offset * offset) * inside).astype(jnp.bfloat16)

    bell_row = window_of(arrived[0], grid_rows)
    bell_col = window_of(arrived[1], grid_cols)
    spread = lax.dot_general(
        bell_row, bell_col, (((0,), (0,)), ((), ())), preferred_element_type=jnp.float32
    )
    field = macro_density + spread
    for sweep in range(STEPS):
        padded = extended(field, (("row", 0), ("col", 1)), 1)
        field = diffuse(padded)
    return (solution, field)


def solution(mesh):
    return jax.shard_map(
        per_device,
        mesh=mesh,
        in_specs=(
            P(("row", "col"), None, None),
            P(("row", "col"), None),
            P(("row", "col"), None, None, None),
            P(("row", "col"), None),
            P(("row", "col"), None),
            P(("row", "col")),
            P(("row", "col")),
            P("row", "col"),
        ),
        out_specs=(P(("row", "col"), None, None), P("row", "col")),
        check_vma=False,
    )
```

profile of v0, /device:TPU:34, one launch (start us, length us, event | category | flops | bytes accessed | tf_op | source)
XLA Modules:
  0.0 727.6 jit_solution(13097304338709061165)
XLA Ops:
  2.6 2.4 collective-permute-start
  6.0 4.1 fusion.113
  10.2 4.5 collective-permute-start.3
  16.6 6.5 collective-permute-done.2
  23.8 7.4 %fusion.48 = f32[8,4,2,256]{3,2,1,0:T(2,128)S(1)} fusion(f32[8,4,256,256]{3,2,1,0:T(8,128)} %param.10, f32[8,4,2,256]{3,2,1,0:T(2,128)S(1)} %bitcast.221, f32[8,4,256]{2,1,0:T(4,128)S(1)} %get-tuple-element.3, f32[8,2,256]{2,1,0:T(2,128)S(1)} %copy-done.4), kind=kOutput, calls=%fused_computation.71 | convolution fusion | flops 50364416 | bytes 8568832 | tf_op jit(solution)/shard_map/bkij,bci->bkcj/dot_general | solution.py:33
  33.6 6.0 collective-permute-start.4
  43.4 2.4 collective-permute-start.7
  45.8 2.6 collective-permute-done.7
  48.4 9.4 %multiply_reduce_fusion.3 = (f32[2]{0:T(128)S(1)}, f32[2]{0:T(128)S(1)}, f32[8,2,256]{2,1,0:T(2,128)S(1)}) fusion(f32[8,2,256]{2,1,0:T(2,128)S(1)} %copy-done.4, f32[8,2,256]{2,1,0:T(2,128)S(1)} %collective-permute-done.7, f32[8,2,256]{2,1,0:T(2,128)S(1)} %collective-permute-done.6, f32[3,8,2,256]{3,2,1,0:T(2,128)S(1)} %fusion.73, ...), kind=kOutput, calls=%fused_computation.168 | convolution fusion | flops 50376700 | bytes 8552464 | tf_op jit(solution)/shard_map/bkij,bkcj->bci/dot_general | solution.py:32
  57.8 65.5 %all-reduce = (f32[2]{0:T(128)S(1)}, f32[2]{0:T(128)S(1)}) all-reduce(f32[2]{0:T(128)S(1)} %get-tuple-element.7, f32[2]{0:T(128)S(1)} %get-tuple-element.6), channel_id=1, replica_groups=mesh['row'=8,'col'=16] {'row','col'}, use_global_device_ids=true, to_apply=%region_1.0 | all-reduce | flops 4 | bytes 32 | tf_op jit(solution)/shard_map/psum | solution.py:110
  123.5 62.4 %psum.44 = f32[2]{0:T(128)S(1)} all-reduce(f32[2]{0:T(128)S(1)} %get-tuple-element.12), channel_id=1, replica_groups=mesh['row'=8,'col'=16] {'row','col'}, use_global_device_ids=true, to_apply=%region_7.8 | all-reduce | flops 2 | bytes 16 | tf_op jit(solution)/shard_map/psum | solution.py:110
  186.0 3.5 collective-permute-start.9
  191.4 3.1 collective-permute-done.8
  194.6 4.2 collective-permute-start.11
  198.8 2.4 collective-permute-start.10
  201.2 5.7 collective-permute-done.10
  207.6 7.4 %fusion.47 = f32[8,4,2,256]{3,2,1,0:T(2,128)S(1)} fusion(f32[8,4,256,256]{3,2,1,0:T(8,128)} %param.10, f32[8,4,2,256]{3,2,1,0:T(2,128)S(1)} %bitcast.219, f32[8,4,256]{2,1,0:T(4,128)S(1)} %get-tuple-element.3, f32[8,2,256]{2,1,0:T(2,128)S(1)} %multiply_add_fusion.2), kind=kOutput, calls=%fused_computation.69 | convolution fusion | flops 50364416 | bytes 8568832 | tf_op jit(solution)/shard_map/bkij,bci->bkcj/dot_general | solution.py:33
  217.4 6.0 collective-permute-start.12
  227.1 2.4 collective-permute-start.15
  229.9 2.3 collective-permute-done.15
  232.2 9.3 %multiply_reduce_fusion.1 = (f32[2]{0:T(128)S(1)}, f32[8,2,256]{2,1,0:T(2,128)S(1)}) fusion(f32[8,2,256]{2,1,0:T(2,128)S(1)} %multiply_add_fusion.2, f32[8,2,256]{2,1,0:T(2,128)S(1)} %collective-permute-done.15, f32[8,2,256]{2,1,0:T(2,128)S(1)} %collective-permute-done.14, f32[3,8,2,256]{3,2,1,0:T(2,128)S(1)} %fusion.71, ...), kind=kOutput, calls=%fused_computation.164 | convolution fusion | flops 50368512 | bytes 8552456 | tf_op jit(solution)/shard_map/bkij,bkcj->bci/dot_general | solution.py:32
  241.5 63.6 %psum.45 = f32[2]{0:T(128)S(1)} all-reduce(f32[2]{0:T(128)S(1)} %get-tuple-element.52), channel_id=1, replica_groups=mesh['row'=8,'col'=16] {'row','col'}, use_global_device_ids=true, to_apply=%region_9.10 | all-reduce | flops 2 | bytes 16 | tf_op jit(solution)/shard_map/psum | solution.py:107
  305.3 62.1 %psum.46 = f32[2]{0:T(128)S(1)} all-reduce(f32[2]{0:T(128)S(1)} %get-tuple-element.10), channel_id=1, replica_groups=mesh['row'=8,'col'=16] {'row','col'}, use_global_device_ids=true, to_apply=%region_11.12 | all-reduce | flops 2 | bytes 16 | tf_op jit(solution)/shard_map/psum | solution.py:110
  367.5 3.8 collective-permute-start.17
  373.4 3.1 collective-permute-done.16
  376.5 4.5 collective-permute-start.19
  381.0 2.1 collective-permute-start.18
  383.5 5.6 collective-permute-done.18
  389.8 7.4 %fusion.46 = f32[8,4,2,256]{3,2,1,0:T(2,128)S(1)} fusion(f32[8,4,256,256]{3,2,1,0:T(8,128)} %param.10, f32[8,4,2,256]{3,2,1,0:T(2,128)S(1)} %bitcast.217, f32[8,4,256]{2,1,0:T(4,128)S(1)} %get-tuple-element.3, f32[8,2,256]{2,1,0:T(2,128)S(1)} %multiply_add_fusion.1), kind=kOutput, calls=%fused_computation.67 | convolution fusion | flops 50364416 | bytes 8568832 | tf_op jit(solution)/shard_map/bkij,bci->bkcj/dot_general | solution.py:33
  399.6 6.0 collective-permute-start.20
  409.3 2.4 collective-permute-start.23
  411.8 2.6 collective-permute-done.23
  414.4 9.3 %fusion.99 = f32[2]{0:T(128)S(1)} fusion(f32[8,2,256]{2,1,0:T(2,128)S(1)} %multiply_add_fusion.1, f32[8,2,256]{2,1,0:T(2,128)S(1)} %collective-permute-done.23, f32[8,2,256]{2,1,0:T(2,128)S(1)} %collective-permute-done.22, f32[3,8,2,256]{3,2,1,0:T(2,128)S(1)} %fusion.69, f32[8,4,2,256]{3,2,1,0:T(2,128)S(1)} %bitcast.218, f32[8,4,256,256]{3,2,1,0:T(8,128)} %param.10, ...), kind=kOutput, calls=%fused_computation.160 | convolution fusion | flops 50368512 | bytes 8536072 | tf_op jit(solution)/shard_map/bkij,bkcj->bci/dot_general | solution.py:32
  423.7 63.6 %psum.47 = f32[2]{0:T(128)S(1)} all-reduce(f32[2]{0:T(128)S(1)} %fusion.99), channel_id=1, replica_groups=mesh['row'=8,'col'=16] {'row','col'}, use_global_device_ids=true, to_apply=%region_13.14 | all-reduce | flops 2 | bytes 16 | tf_op jit(solution)/shard_map/psum | solution.py:107
  487.9 6.1 scatter_custom_fusion
  495.5 6.9 all-to-all-start
  502.4 8.2 %all-to-all-done = f32[2,128,32]{2,0,1:T(2,128)S(1)} async-done(((f32[2,128,32]{2,0,1:T(2,128)}), f32[2,128,32]{2,0,1:T(2,128)S(1)}, u32[]{:S(2)}, u32[]{:S(2)}) %all-to-all-start) | async-done | bytes 32800 | tf_op jit(solution)/shard_map/all_to_all | solution.py:125
  511.2 22.2 %fusion.41 = f32[2048,512]{1,0:T(8,128)S(1)} fusion(f32[2048,512]{1,0:T(8,128)} %param.15, f32[4096]{0:T(1024)S(1)} %squeeze.82, f32[512]{0:T(512)S(1)} %iota_convert_fusion.1, s32[4096]{0:T(1024)S(1)} %get-tuple-element.48, s32[4096]{0:T(1024)S(1)} %get-tuple-element.47, f32[4096]{0:T(1024)S(1)} %squeeze.81, f32[2048]{0:T(1024)S(1)} %iota_convert_fusion, ...), kind=kOutput, calls=%fused_computation.65 | convolution fusion | flops 8674869248 | bytes 8497152 | tf_op jit(solution)/shard_map/dot_general | solution.py:147
  535.4 2.4 collective-permute-start.24
  539.8 3.0 collective-permute-done.25
  542.7 13.5 %concatenate.90 = f32[2050,512]{1,0:T(8,128)} concatenate(f32[1,512]{1,0:T(1,128)S(1)} %collective-permute-done.25, f32[2048,512]{1,0:T(8,128)} %copy-done.3, f32[1,512]{1,0:T(1,128)S(1)} %collective-permute-done.24), dimensions={0} | concatenate | bytes 8396800 | tf_op jit(solution)/shard_map/concatenate | solution.py:27
  558.5 3.8 collective-permute-start.26
  562.7 2.1 collective-permute-start.27
  565.1 5.2 collective-permute-done.27
  570.7 12.7 %fusion.32 = f32[2048,512]{1,0:T(8,128)S(1)} fusion(f32[2048,512]{1,0:T(8,128)} %copy-done.3, f32[2050,512]{1,0:T(8,128)} %concatenate.90, f32[2050,1]{1,0:T(8,128)S(1)} %copy.61, f32[2050,1]{1,0:T(8,128)S(1)} %copy.59, f32[1,512]{1,0:T(1,128)S(1)} %collective-permute-done.25, f32[1,512]{1,0:T(1,128)S(1)} %collective-permute-done.24), kind=kLoop, calls=%fused_computation.53 | loop fusion | flops 11534336 | bytes 12607504 | tf_op jit(solution)/shard_map/add | solution.py:41
  587.4 2.4 collective-permute-start.29
  589.8 2.5 collective-permute-done.29
  592.3 13.5 %concatenate.95 = f32[2050,512]{1,0:T(8,128)} concatenate(f32[1,512]{1,0:T(1,128)S(1)} %collective-permute-done.29, f32[2048,512]{1,0:T(8,128)} %copy-done, f32[1,512]{1,0:T(1,128)S(1)} %collective-permute-done.28), dimensions={0} | concatenate | bytes 8396800 | tf_op jit(solution)/shard_map/concatenate | solution.py:27
  610.4 3.9 collective-permute-start.31
  614.7 3.3 collective-permute-done.31
  618.4 12.5 %fusion.26 = f32[2048,512]{1,0:T(8,128)S(1)} fusion(f32[2048,512]{1,0:T(8,128)} %copy-done, f32[2050,512]{1,0:T(8,128)} %concatenate.95, f32[2050,1]{1,0:T(8,128)S(1)} %copy.65, f32[2050,1]{1,0:T(8,128)S(1)} %copy.63, f32[1,512]{1,0:T(1,128)S(1)} %collective-permute-done.29, f32[1,512]{1,0:T(1,128)S(1)} %collective-permute-done.28), kind=kLoop, calls=%fused_computation.43 | loop fusion | flops 11534336 | bytes 12607504 | tf_op jit(solution)/shard_map/add | solution.py:41
  634.9 2.4 collective-permute-start.33
  637.3 2.5 collective-permute-done.33
  639.8 13.5 %concatenate.100 = f32[2050,512]{1,0:T(8,128)} concatenate(f32[1,512]{1,0:T(1,128)S(1)} %collective-permute-done.33, f32[2048,512]{1,0:T(8,128)} %copy-done.1, f32[1,512]{1,0:T(1,128)S(1)} %collective-permute-done.32), dimensions={0} | concatenate | bytes 8396800 | tf_op jit(solution)/shard_map/concatenate | solution.py:27
  657.9 3.9 collective-permute-start.35
  662.2 3.3 collective-permute-done.35
  665.9 12.5 %fusion.20 = f32[2048,512]{1,0:T(8,128)S(1)} fusion(f32[2048,512]{1,0:T(8,128)} %copy-done.1, f32[2050,512]{1,0:T(8,128)} %concatenate.100, f32[2050,1]{1,0:T(8,128)S(1)} %copy.69, f32[2050,1]{1,0:T(8,128)S(1)} %copy.67, f32[1,512]{1,0:T(1,128)S(1)} %collective-permute-done.33, f32[1,512]{1,0:T(1,128)S(1)} %collective-permute-done.32), kind=kLoop, calls=%fused_computation.33 | loop fusion | flops 11534336 | bytes 12607504 | tf_op jit(solution)/shard_map/add | solution.py:41
  682.4 2.4 collective-permute-start.37
  684.8 2.5 collective-permute-done.37
  687.3 13.5 %concatenate.105 = f32[2050,512]{1,0:T(8,128)} concatenate(f32[1,512]{1,0:T(1,128)S(1)} %collective-permute-done.37, f32[2048,512]{1,0:T(8,128)} %copy-done.2, f32[1,512]{1,0:T(1,128)S(1)} %collective-permute-done.36), dimensions={0} | concatenate | bytes 8396800 | tf_op jit(solution)/shard_map/concatenate | solution.py:27
  703.1 2.2 collective-permute-start.38
  705.6 3.9 collective-permute-start.39
  709.9 3.3 collective-permute-done.39
  713.6 13.7 %fusion.14 = f32[2048,512]{1,0:T(8,128)} fusion(f32[2048,512]{1,0:T(8,128)} %copy-done.2, f32[2050,512]{1,0:T(8,128)} %concatenate.105, f32[2050,1]{1,0:T(8,128)S(1)} %copy.73, f32[2050,1]{1,0:T(8,128)S(1)} %copy.71, f32[1,512]{1,0:T(1,128)S(1)} %collective-permute-done.37, f32[1,512]{1,0:T(1,128)S(1)} %collective-permute-done.36), kind=kLoop, calls=%fused_computation.23 | loop fusion | flops 11534336 | bytes 12607504 | tf_op jit(solution)/shard_map/add | solution.py:41
  (155 shorter events, 65.7 us)
Async XLA Ops:
  0.6 9.5 %collective-permute-start.1 = (f32[1,1,8,2,256]{4,3,2,1,0:T(2,128)}, f32[1,1,8,2,256]{4,3,2,1,0:T(2,128)S(1)}, u32[]{:S(2)}, u32[]{:S(2)}) collective-permute-start(f32[1,1,8,2,256]{4,3,2,1,0:T(2,128)} %bitcast.209), channel_id=1, source_target_pairs={{16,0},{32,16},{48,32},{64,48},{80,64},{96,80},{112,96},{17,1},{33... | collective-permute-start | bytes 49160 | tf_op jit(solution)/shard_map/ppermute | solution.py:26
  2.6 7.6 %collective-permute-start = (f32[1,1,8,2,256]{4,3,2,1,0:T(2,128)}, f32[1,1,8,2,256]{4,3,2,1,0:T(2,128)S(1)}, u32[]{:S(2)}, u32[]{:S(2)}) collective-permute-start(f32[1,1,8,2,256]{4,3,2,1,0:T(2,128)} %bitcast.210), channel_id=1, source_target_pairs={{0,16},{16,32},{32,48},{48,64},{64,80},{80,96},{96,112},{1,17},{17... | collective-permute-start | bytes 49160 | tf_op jit(solution)/shard_map/ppermute | solution.py:25
  6.0 4.2 copy-start.4
  10.2 6.4 collective-permute-start.3
  14.6 8.5 %collective-permute-start.2 = (f32[3,1,8,2,256]{4,3,2,1,0:T(2,128)S(1)}, f32[3,1,8,2,256]{4,3,2,1,0:T(2,128)S(1)}, u32[]{:S(2)}, u32[]{:S(2)}) collective-permute-start(f32[3,1,8,2,256]{4,3,2,1,0:T(2,128)S(1)} %pad_maximum_fusion.19), channel_id=1, source_target_pairs={{0,1},{1,2},{2,3},{3,4},{4,5},{5,6},{6,7},{7,8},{8,9},{9,10},{10,1... | collective-permute-start | bytes 147464 | tf_op jit(solution)/shard_map/ppermute | solution.py:25
  23.8 24.6 %copy-start.6 = (f32[8,256]{1,0:T(8,128)S(1)}, f32[8,256]{1,0:T(8,128)}, u32[]{:S(2)}) copy-start(f32[8,256]{1,0:T(8,128)} %param.9) | copy-start | bytes 24580
  31.7 8.1 %collective-permute-start.5 = (f32[3,8,2,256]{3,2,1,0:T(2,128)S(1)}, f32[3,8,2,256]{3,2,1,0:T(2,128)S(1)}, u32[]{:S(2)}, u32[]{:S(2)}) collective-permute-start(f32[3,8,2,256]{3,2,1,0:T(2,128)S(1)} %bitcast.247), channel_id=1, source_target_pairs={{0,1},{1,2},{2,3},{3,4},{4,5},{5,6},{6,7},{7,8},{8,9},{9,10},{10,1... | collective-permute-start | bytes 147464 | tf_op jit(solution)/shard_map/ppermute | solution.py:15
  33.6 7.8 %collective-permute-start.4 = (f32[3,8,2,256]{3,2,1,0:T(2,128)S(1)}, f32[3,8,2,256]{3,2,1,0:T(2,128)S(1)}, u32[]{:S(2)}, u32[]{:S(2)}) collective-permute-start(f32[3,8,2,256]{3,2,1,0:T(2,128)S(1)} %bitcast.244), channel_id=1, source_target_pairs={{1,0},{2,1},{3,2},{4,3},{5,4},{6,5},{7,6},{8,7},{9,8},{10,9},{11,1... | collective-permute-start | bytes 147464 | tf_op jit(solution)/shard_map/ppermute | solution.py:15
  41.4 4.3 collective-permute-start.6
  43.4 5.1 collective-permute-start.7
  186.0 5.4 collective-permute-start.9
  189.5 5.1 collective-permute-start.8
  194.6 6.6 collective-permute-start.11
  198.8 8.1 %collective-permute-start.10 = (f32[3,1,8,2,256]{4,3,2,1,0:T(2,128)S(1)}, f32[3,1,8,2,256]{4,3,2,1,0:T(2,128)S(1)}, u32[]{:S(2)}, u32[]{:S(2)}) collective-permute-start(f32[3,1,8,2,256]{4,3,2,1,0:T(2,128)S(1)} %pad_maximum_fusion.20), channel_id=1, source_target_pairs={{0,1},{1,2},{2,3},{3,4},{4,5},{5,6},{6,7},{7,8},{8,9},{9,10},{10,1... | collective-permute-start | bytes 147464 | tf_op jit(solution)/shard_map/ppermute | solution.py:25
  207.6 15.8 %copy-start.5 = (s32[2048,1]{0,1:T(1,128)S(1)}, s32[2048,1]{0,1:T(1,128)}, u32[]{:S(2)}) copy-start(s32[2048,1]{0,1:T(1,128)} %param.12) | copy-start | bytes 24580
  215.5 8.1 %collective-permute-start.13 = (f32[3,8,2,256]{3,2,1,0:T(2,128)S(1)}, f32[3,8,2,256]{3,2,1,0:T(2,128)S(1)}, u32[]{:S(2)}, u32[]{:S(2)}) collective-permute-start(f32[3,8,2,256]{3,2,1,0:T(2,128)S(1)} %bitcast.246), channel_id=1, source_target_pairs={{0,1},{1,2},{2,3},{3,4},{4,5},{5,6},{6,7},{7,8},{8,9},{9,10},{10,1... | collective-permute-start | bytes 147464 | tf_op jit(solution)/shard_map/ppermute | solution.py:15
  217.4 7.8 %collective-permute-start.12 = (f32[3,8,2,256]{3,2,1,0:T(2,128)S(1)}, f32[3,8,2,256]{3,2,1,0:T(2,128)S(1)}, u32[]{:S(2)}, u32[]{:S(2)}) collective-permute-start(f32[3,8,2,256]{3,2,1,0:T(2,128)S(1)} %bitcast.243), channel_id=1, source_target_pairs={{1,0},{2,1},{3,2},{4,3},{5,4},{6,5},{7,6},{8,7},{9,8},{10,9},{11,1... | collective-permute-start | bytes 147464 | tf_op jit(solution)/shard_map/ppermute | solution.py:15
  225.2 4.7 collective-permute-start.14
  227.1 5.1 collective-permute-start.15
  367.5 5.8 collective-permute-start.17
  371.4 5.1 collective-permute-start.16
  376.5 7.1 collective-permute-start.19
  381.0 8.1 %collective-permute-start.18 = (f32[3,1,8,2,256]{4,3,2,1,0:T(2,128)S(1)}, f32[3,1,8,2,256]{4,3,2,1,0:T(2,128)S(1)}, u32[]{:S(2)}, u32[]{:S(2)}) collective-permute-start(f32[3,1,8,2,256]{4,3,2,1,0:T(2,128)S(1)} %pad_maximum_fusion.21), channel_id=1, source_target_pairs={{0,1},{1,2},{2,3},{3,4},{4,5},{5,6},{6,7},{7,8},{8,9},{9,10},{10,1... | collective-permute-start | bytes 147464 | tf_op jit(solution)/shard_map/ppermute | solution.py:25
  397.7 8.6 %collective-permute-start.21 = (f32[3,8,2,256]{3,2,1,0:T(2,128)S(1)}, f32[3,8,2,256]{3,2,1,0:T(2,128)S(1)}, u32[]{:S(2)}, u32[]{:S(2)}) collective-permute-start(f32[3,8,2,256]{3,2,1,0:T(2,128)S(1)} %bitcast.245), channel_id=1, source_target_pairs={{0,1},{1,2},{2,3},{3,4},{4,5},{5,6},{6,7},{7,8},{8,9},{9,10},{10,1... | collective-permute-start | bytes 147464 | tf_op jit(solution)/shard_map/ppermute | solution.py:15
  399.6 7.8 %collective-permute-start.20 = (f32[3,8,2,256]{3,2,1,0:T(2,128)S(1)}, f32[3,8,2,256]{3,2,1,0:T(2,128)S(1)}, u32[]{:S(2)}, u32[]{:S(2)}) collective-permute-start(f32[3,8,2,256]{3,2,1,0:T(2,128)S(1)} %bitcast.242), channel_id=1, source_target_pairs={{1,0},{2,1},{3,2},{4,3},{5,4},{6,5},{7,6},{8,7},{9,8},{10,9},{11,1... | collective-permute-start | bytes 147464 | tf_op jit(solution)/shard_map/ppermute | solution.py:15
  407.4 4.4 collective-permute-start.22
  409.3 5.1 collective-permute-start.23
  411.8 75.7 %copy-start.8 = (s32[2048]{0:T(1024)S(1)}, s32[2048]{0:T(1024)}, u32[]{:S(2)}) copy-start(s32[2048]{0:T(1024)} %param.13) | copy-start | bytes 24580
  411.8 75.7 %copy-start.9 = (s32[2048]{0:T(1024)S(1)}, s32[2048]{0:T(1024)}, u32[]{:S(2)}) copy-start(s32[2048]{0:T(1024)} %param.14) | copy-start | bytes 24580
  487.4 45.9 %copy-start.7 = (f32[8,2,256]{2,1,0:T(2,128)}, f32[8,2,256]{2,1,0:T(2,128)S(1)}, u32[]{:S(2)}) copy-start(f32[8,2,256]{2,1,0:T(2,128)S(1)} %multiply_add_fusion) | copy-start | bytes 49156
  495.5 15.1 %all-to-all-start = ((f32[2,128,32]{2,0,1:T(2,128)}), f32[2,128,32]{2,0,1:T(2,128)S(1)}, u32[]{:S(2)}, u32[]{:S(2)}) async-start(f32[2,128,32]{2,0,1:T(2,128)} %copy.57), calls=%async_computation | async-start | bytes 262144 | tf_op jit(solution)/shard_map/all_to_all | solution.py:125
  533.3 2.0 copy-start.3
  535.4 4.4 collective-permute-start.24
  537.8 4.9 collective-permute-start.25
  558.5 6.2 collective-permute-start.26
  562.7 7.7 %collective-permute-start.27 = (f32[2050,1]{0,1:T(1,128)S(1)}, f32[2050,1]{0,1:T(1,128)S(1)}, u32[]{:S(2)}, u32[]{:S(2)}) collective-permute-start(f32[2050,1]{0,1:T(1,128)S(1)} %copy.60), channel_id=1, source_target_pairs={{0,1},{1,2},{2,3},{3,4},{4,5},{5,6},{6,7},{7,8},{8,9},{9,10},{10,1... | collective-permute-start | bytes 24608 | tf_op jit(solution)/shard_map/ppermute | solution.py:25
  583.5 2.0 copy-start
  585.5 4.3 collective-permute-start.28
  587.4 4.9 collective-permute-start.29
  608.1 6.2 collective-permute-start.30
  610.4 7.7 %collective-permute-start.31 = (f32[2050,1]{0,1:T(1,128)S(1)}, f32[2050,1]{0,1:T(1,128)S(1)}, u32[]{:S(2)}, u32[]{:S(2)}) collective-permute-start(f32[2050,1]{0,1:T(1,128)S(1)} %copy.64), channel_id=1, source_target_pairs={{0,1},{1,2},{2,3},{3,4},{4,5},{5,6},{6,7},{7,8},{8,9},{9,10},{10,1... | collective-permute-start | bytes 24608 | tf_op jit(solution)/shard_map/ppermute | solution.py:25
  631.0 2.0 copy-start.1
  633.0 4.3 collective-permute-start.32
  634.9 4.9 collective-permute-start.33
  655.6 6.2 collective-permute-start.34
  657.9 7.7 %collective-permute-start.35 = (f32[2050,1]{0,1:T(1,128)S(1)}, f32[2050,1]{0,1:T(1,128)S(1)}, u32[]{:S(2)}, u32[]{:S(2)}) collective-permute-start(f32[2050,1]{0,1:T(1,128)S(1)} %copy.68), channel_id=1, source_target_pairs={{0,1},{1,2},{2,3},{3,4},{4,5},{5,6},{6,7},{7,8},{8,9},{9,10},{10,1... | collective-permute-start | bytes 24608 | tf_op jit(solution)/shard_map/ppermute | solution.py:25
  678.5 2.0 copy-start.2
  680.5 4.3 collective-permute-start.36
  682.4 4.9 collective-permute-start.37
  703.1 6.5 collective-permute-start.38
  705.6 7.7 %collective-permute-start.39 = (f32[2050,1]{0,1:T(1,128)S(1)}, f32[2050,1]{0,1:T(1,128)S(1)}, u32[]{:S(2)}, u32[]{:S(2)}) collective-permute-start(f32[2050,1]{0,1:T(1,128)S(1)} %copy.72), channel_id=1, source_target_pairs={{0,1},{1,2},{2,3},{3,4},{4,5},{5,6},{6,7},{7,8},{8,9},{9,10},{10,1... | collective-permute-start | bytes 24608 | tf_op jit(solution)/shard_map/ppermute | solution.py:25
where the time goes:
time: 739 us; the launch traced here: 728 us
  blocking collectives  317 us (43%)
  starting transfers between devices  120 us (16%)
  local copies, waits for them, and re-layouts  87.6 us (12%)
  matrix products  73.3 us (10%)
  waiting for transfers between devices  69.9 us (9%)
  other arithmetic  57.9 us (8%)
    psum x3, blocking collectives, norm_of(): return lax.psum(jnp.sum(resid * resid, axis=(0, 2)), ('row', 'col'))  190 us
    psum x2, blocking collectives, curve_of(): return lax.psum(jnp.sum(direction * image, axis=(0, 2)), ('row', 'col'))  127 us
    concatenate x4, local copies, waits for them, and re-layouts, extended(): value = jnp.concatenate([before, value, after], axis=dim)  54.2 us
    add x4, other arithmetic, diffuse(): centre + RATE * (padded[2:, 1:-1] + padded[:-2, 1:-1] + padded[1:-1, 2:]...  51.5 us
    ppermute x14, waiting for transfers between devices, extended(): before = lax.ppermute(last, axis, up)  49.6 us
    ppermute x14, starting transfers between devices, extended(): after = lax.ppermute(leading, axis, down)  40.5 us
    ppermute x12, starting transfers between devices, passed_along(): return lax.ppermute(block, axis, route)  36.8 us
    ppermute x14, starting transfers between devices, extended(): before = lax.ppermute(last, axis, up)  35.7 us
  transfers between devices with their start and end apart: 41, of which 21 were waited for; matrix products, arithmetic and copies ran while one was open for 1% of the time, Pallas kernels for 0%

commit v1 on v0

--- a/solution.py
+++ b/solution.py
@@ -107,7 +107,7 @@
         return lax.psum(jnp.sum(direction * image, axis=(0, 2)), ("row", "col"))
 
     def norm_of(resid):
-        return lax.psum(jnp.sum(resid * resid, axis=(0, 2)), ("row", "col"))
+        return jnp.sum(lax.all_gather(jnp.sum(resid * resid, axis=(0, 2)), ("row", "col")), axis=0)
 
     solution = run_solver(image_of, curve_of, norm_of, right_side)
     clusters_own = blocks_own * width_tile

time: 739 us -> 740 us (level)
    unnamed x0 -> x3, blocking collectives: none -> 190 us
    psum x3 -> x0, blocking collectives: 190 us -> none  [norm_of(): return lax.psum(jnp.sum(resid * resid, axis=(0, 2)), ('row', 'col'))]
where the time goes in v1:
time: 740 us; the launch traced here: 729 us
  blocking collectives  318 us (43%)
  starting transfers between devices  119 us (16%)
  local copies, waits for them, and re-layouts  88.5 us (12%)
  matrix products  73.1 us (10%)
  waiting for transfers between devices  70.5 us (10%)
  other arithmetic  58.1 us (8%)
    unnamed x3, blocking collectives  190 us
    psum x2, blocking collectives, curve_of(): return lax.psum(jnp.sum(direction * image, axis=(0, 2)), ('row', 'col'))  127 us
    concatenate x4, local copies, waits for them, and re-layouts, extended(): value = jnp.concatenate([before, value, after], axis=dim)  53.9 us
    add x4, other arithmetic, diffuse(): centre + RATE * (padded[2:, 1:-1] + padded[:-2, 1:-1] + padded[1:-1, 2:]...  51.5 us
    ppermute x14, waiting for transfers between devices, extended(): before = lax.ppermute(last, axis, up)  50.2 us
    ppermute x14, starting transfers between devices, extended(): after = lax.ppermute(leading, axis, down)  40.4 us
    ppermute x12, starting transfers between devices, passed_along(): return lax.ppermute(block, axis, route)  36.8 us
    ppermute x14, starting transfers between devices, extended(): before = lax.ppermute(last, axis, up)  35 us
  transfers between devices with their start and end apart: 41, of which 21 were waited for; matrix products, arithmetic and copies ran while one was open for 1% of the time, Pallas kernels for 0%

profile of v1, /device:TPU:34, one launch (start us, length us, event | category | flops | bytes accessed | tf_op | source)
XLA Modules:
  0.0 728.8 jit_solution(15709327341588858457)
XLA Ops:
  2.6 2.4 collective-permute-start
  6.0 4.1 fusion.113
  10.2 4.5 collective-permute-start.3
  16.6 6.5 collective-permute-done.2
  23.8 7.4 %fusion.48 = f32[8,4,2,256]{3,2,1,0:T(2,128)S(1)} fusion(f32[8,4,256,256]{3,2,1,0:T(8,128)} %param.10, f32[8,4,2,256]{3,2,1,0:T(2,128)S(1)} %bitcast.217, f32[8,4,256]{2,1,0:T(4,128)S(1)} %get-tuple-element.3, f32[8,2,256]{2,1,0:T(2,128)S(1)} %copy-done.4), kind=kOutput, calls=%fused_computation.71 | convolution fusion | flops 50364416 | bytes 8568832 | tf_op jit(solution)/shard_map/bkij,bci->bkcj/dot_general | solution.py:33
  33.6 6.0 collective-permute-start.4
  43.4 2.4 collective-permute-start.7
  45.8 2.6 collective-permute-done.7
  48.4 9.4 %multiply_reduce_fusion.3 = (f32[2]{0:T(128)S(1)}, f32[2]{0:T(128)S(1)}, f32[8,2,256]{2,1,0:T(2,128)S(1)}) fusion(f32[8,2,256]{2,1,0:T(2,128)S(1)} %copy-done.4, f32[8,2,256]{2,1,0:T(2,128)S(1)} %collective-permute-done.7, f32[8,2,256]{2,1,0:T(2,128)S(1)} %collective-permute-done.6, f32[3,8,2,256]{3,2,1,0:T(2,128)S(1)} %fusion.73, ...), kind=kOutput, calls=%fused_computation.168 | convolution fusion | flops 50376700 | bytes 8552464 | tf_op jit(solution)/shard_map/bkij,bkcj->bci/dot_general | solution.py:32
  58.1 65.4 %all-reduce.3 = (f32[256]{0:T(256)S(1)}, f32[2]{0:T(128)S(1)}) all-reduce(f32[256]{0:T(256)S(1)} %dynamic-update-slice, f32[2]{0:T(128)S(1)} %get-tuple-element.6), channel_id=2, replica_groups=mesh['row'=8,'col'=16] {'row','col'}, use_global_device_ids=true, to_apply=%add | all-reduce | flops 258 | bytes 2064
  124.1 62.5 %all-reduce.1 = f32[256]{0:T(256)S(1)} all-reduce(f32[256]{0:T(256)S(1)} %dynamic-update-slice.1), channel_id=3, replica_groups=mesh['row'=8,'col'=16] {'row','col'}, use_global_device_ids=true, to_apply=%add.1 | all-reduce | flops 256 | bytes 2048
  186.9 3.5 collective-permute-start.9
  192.4 3.1 collective-permute-done.8
  195.5 4.2 collective-permute-start.11
  201.7 6.2 collective-permute-done.10
  208.6 7.4 %fusion.47 = f32[8,4,2,256]{3,2,1,0:T(2,128)S(1)} fusion(f32[8,4,256,256]{3,2,1,0:T(8,128)} %param.10, f32[8,4,2,256]{3,2,1,0:T(2,128)S(1)} %bitcast.221, f32[8,4,256]{2,1,0:T(4,128)S(1)} %get-tuple-element.3, f32[8,2,256]{2,1,0:T(2,128)S(1)} %multiply_add_fusion.2), kind=kOutput, calls=%fused_computation.69 | convolution fusion | flops 50364416 | bytes 8568832 | tf_op jit(solution)/shard_map/bkij,bci->bkcj/dot_general | solution.py:33
  218.3 6.0 collective-permute-start.12
  228.1 2.4 collective-permute-start.15
  230.9 2.3 collective-permute-done.15
  233.1 9.3 %multiply_reduce_fusion.1 = (f32[2]{0:T(128)S(1)}, f32[8,2,256]{2,1,0:T(2,128)S(1)}) fusion(f32[8,2,256]{2,1,0:T(2,128)S(1)} %multiply_add_fusion.2, f32[8,2,256]{2,1,0:T(2,128)S(1)} %collective-permute-done.15, f32[8,2,256]{2,1,0:T(2,128)S(1)} %collective-permute-done.14, f32[3,8,2,256]{3,2,1,0:T(2,128)S(1)} %fusion.71, ...), kind=kOutput, calls=%fused_computation.164 | convolution fusion | flops 50368512 | bytes 8552456 | tf_op jit(solution)/shard_map/bkij,bkcj->bci/dot_general | solution.py:32
  242.5 63.6 %psum.22 = f32[2]{0:T(128)S(1)} all-reduce(f32[2]{0:T(128)S(1)} %get-tuple-element.52), channel_id=1, replica_groups=mesh['row'=8,'col'=16] {'row','col'}, use_global_device_ids=true, to_apply=%region_9.10 | all-reduce | flops 2 | bytes 16 | tf_op jit(solution)/shard_map/psum | solution.py:107
  306.5 62.5 %all-reduce.2 = f32[256]{0:T(256)S(1)} all-reduce(f32[256]{0:T(256)S(1)} %dynamic-update-slice.2), channel_id=4, replica_groups=mesh['row'=8,'col'=16] {'row','col'}, use_global_device_ids=true, to_apply=%add.2 | all-reduce | flops 256 | bytes 2048
  369.3 3.8 collective-permute-start.17
  375.1 3.1 collective-permute-done.16
  378.2 4.5 collective-permute-start.19
  385.1 5.7 collective-permute-done.18
  391.6 7.4 %fusion.46 = f32[8,4,2,256]{3,2,1,0:T(2,128)S(1)} fusion(f32[8,4,256,256]{3,2,1,0:T(8,128)} %param.10, f32[8,4,2,256]{3,2,1,0:T(2,128)S(1)} %bitcast.219, f32[8,4,256]{2,1,0:T(4,128)S(1)} %get-tuple-element.3, f32[8,2,256]{2,1,0:T(2,128)S(1)} %multiply_add_fusion.1), kind=kOutput, calls=%fused_computation.67 | convolution fusion | flops 50364416 | bytes 8568832 | tf_op jit(solution)/shard_map/bkij,bci->bkcj/dot_general | solution.py:33
  401.3 6.0 collective-permute-start.20
  411.1 2.4 collective-permute-start.23
  413.6 2.6 collective-permute-done.23
  416.1 9.3 %fusion.99 = f32[2]{0:T(128)S(1)} fusion(f32[8,2,256]{2,1,0:T(2,128)S(1)} %multiply_add_fusion.1, f32[8,2,256]{2,1,0:T(2,128)S(1)} %collective-permute-done.23, f32[8,2,256]{2,1,0:T(2,128)S(1)} %collective-permute-done.22, f32[3,8,2,256]{3,2,1,0:T(2,128)S(1)} %fusion.69, f32[8,4,2,256]{3,2,1,0:T(2,128)S(1)} %bitcast.220, f32[8,4,256,256]{3,2,1,0:T(8,128)} %param.10, ...), kind=kOutput, calls=%fused_computation.160 | convolution fusion | flops 50368512 | bytes 8536072 | tf_op jit(solution)/shard_map/bkij,bkcj->bci/dot_general | solution.py:32
  425.5 63.6 %psum.23 = f32[2]{0:T(128)S(1)} all-reduce(f32[2]{0:T(128)S(1)} %fusion.99), channel_id=1, replica_groups=mesh['row'=8,'col'=16] {'row','col'}, use_global_device_ids=true, to_apply=%region_13.14 | all-reduce | flops 2 | bytes 16 | tf_op jit(solution)/shard_map/psum | solution.py:107
  489.6 6.1 scatter_custom_fusion
  497.2 6.8 all-to-all-start
  504.1 8.3 %all-to-all-done = f32[2,128,32]{2,0,1:T(2,128)S(1)} async-done(((f32[2,128,32]{2,0,1:T(2,128)}), f32[2,128,32]{2,0,1:T(2,128)S(1)}, u32[]{:S(2)}, u32[]{:S(2)}) %all-to-all-start) | async-done | bytes 32800 | tf_op jit(solution)/shard_map/all_to_all | solution.py:125
  512.9 22.0 %fusion.41 = f32[2048,512]{1,0:T(8,128)S(1)} fusion(f32[2048,512]{1,0:T(8,128)} %param.15, f32[4096]{0:T(1024)S(1)} %squeeze.82, f32[512]{0:T(512)S(1)} %iota_convert_fusion.1, s32[4096]{0:T(1024)S(1)} %get-tuple-element.48, s32[4096]{0:T(1024)S(1)} %get-tuple-element.47, f32[4096]{0:T(1024)S(1)} %squeeze.81, f32[2048]{0:T(1024)S(1)} %iota_convert_fusion, ...), kind=kOutput, calls=%fused_computation.65 | convolution fusion | flops 8674869248 | bytes 8497152 | tf_op jit(solution)/shard_map/dot_general | solution.py:147
  534.9 2.0 copy-done.3
  536.9 2.4 collective-permute-start.24
  541.3 3.0 collective-permute-done.25
  544.3 13.5 %concatenate.90 = f32[2050,512]{1,0:T(8,128)} concatenate(f32[1,512]{1,0:T(1,128)S(1)} %collective-permute-done.25, f32[2048,512]{1,0:T(8,128)} %copy-done.3, f32[1,512]{1,0:T(1,128)S(1)} %collective-permute-done.24), dimensions={0} | concatenate | bytes 8396800 | tf_op jit(solution)/shard_map/concatenate | solution.py:27
  560.0 3.8 collective-permute-start.26
  564.2 2.1 collective-permute-start.27
  566.6 5.2 collective-permute-done.27
  572.2 12.9 %fusion.32 = f32[2048,512]{1,0:T(8,128)S(1)} fusion(f32[2048,512]{1,0:T(8,128)} %copy-done.3, f32[2050,512]{1,0:T(8,128)} %concatenate.90, f32[2050,1]{1,0:T(8,128)S(1)} %copy.61, f32[2050,1]{1,0:T(8,128)S(1)} %copy.59, f32[1,512]{1,0:T(1,128)S(1)} %collective-permute-done.25, f32[1,512]{1,0:T(1,128)S(1)} %collective-permute-done.24), kind=kLoop, calls=%fused_computation.53 | loop fusion | flops 11534336 | bytes 12607504 | tf_op jit(solution)/shard_map/add | solution.py:41
  585.1 2.0 copy-done
  589.0 2.4 collective-permute-start.29
  591.4 2.5 collective-permute-done.29
  593.9 13.5 %concatenate.95 = f32[2050,512]{1,0:T(8,128)} concatenate(f32[1,512]{1,0:T(1,128)S(1)} %collective-permute-done.29, f32[2048,512]{1,0:T(8,128)} %copy-done, f32[1,512]{1,0:T(1,128)S(1)} %collective-permute-done.28), dimensions={0} | concatenate | bytes 8396800 | tf_op jit(solution)/shard_map/concatenate | solution.py:27
  611.9 3.9 collective-permute-start.31
  616.3 3.3 collective-permute-done.31
  620.0 12.5 %fusion.26 = f32[2048,512]{1,0:T(8,128)S(1)} fusion(f32[2048,512]{1,0:T(8,128)} %copy-done, f32[2050,512]{1,0:T(8,128)} %concatenate.95, f32[2050,1]{1,0:T(8,128)S(1)} %copy.65, f32[2050,1]{1,0:T(8,128)S(1)} %copy.63, f32[1,512]{1,0:T(1,128)S(1)} %collective-permute-done.29, f32[1,512]{1,0:T(1,128)S(1)} %collective-permute-done.28), kind=kLoop, calls=%fused_computation.43 | loop fusion | flops 11534336 | bytes 12607504 | tf_op jit(solution)/shard_map/add | solution.py:41
  636.4 2.4 collective-permute-start.33
  638.8 2.5 collective-permute-done.33
  641.3 13.5 %concatenate.100 = f32[2050,512]{1,0:T(8,128)} concatenate(f32[1,512]{1,0:T(1,128)S(1)} %collective-permute-done.33, f32[2048,512]{1,0:T(8,128)} %copy-done.1, f32[1,512]{1,0:T(1,128)S(1)} %collective-permute-done.32), dimensions={0} | concatenate | bytes 8396800 | tf_op jit(solution)/shard_map/concatenate | solution.py:27
  659.3 3.9 collective-permute-start.35
  663.7 3.3 collective-permute-done.35
  667.4 12.5 %fusion.20 = f32[2048,512]{1,0:T(8,128)S(1)} fusion(f32[2048,512]{1,0:T(8,128)} %copy-done.1, f32[2050,512]{1,0:T(8,128)} %concatenate.100, f32[2050,1]{1,0:T(8,128)S(1)} %copy.69, f32[2050,1]{1,0:T(8,128)S(1)} %copy.67, f32[1,512]{1,0:T(1,128)S(1)} %collective-permute-done.33, f32[1,512]{1,0:T(1,128)S(1)} %collective-permute-done.32), kind=kLoop, calls=%fused_computation.33 | loop fusion | flops 11534336 | bytes 12607504 | tf_op jit(solution)/shard_map/add | solution.py:41
  683.7 2.4 collective-permute-start.37
  686.2 2.5 collective-permute-done.37
  688.6 13.5 %concatenate.105 = f32[2050,512]{1,0:T(8,128)} concatenate(f32[1,512]{1,0:T(1,128)S(1)} %collective-permute-done.37, f32[2048,512]{1,0:T(8,128)} %copy-done.2, f32[1,512]{1,0:T(1,128)S(1)} %collective-permute-done.36), dimensions={0} | concatenate | bytes 8396800 | tf_op jit(solution)/shard_map/concatenate | solution.py:27
  704.4 2.1 collective-permute-start.38
  706.8 3.9 collective-permute-start.39
  711.2 3.3 collective-permute-done.39
  714.9 13.7 %fusion.14 = f32[2048,512]{1,0:T(8,128)} fusion(f32[2048,512]{1,0:T(8,128)} %copy-done.2, f32[2050,512]{1,0:T(8,128)} %concatenate.105, f32[2050,1]{1,0:T(8,128)S(1)} %copy.73, f32[2050,1]{1,0:T(8,128)S(1)} %copy.71, f32[1,512]{1,0:T(1,128)S(1)} %collective-permute-done.37, f32[1,512]{1,0:T(1,128)S(1)} %collective-permute-done.36), kind=kLoop, calls=%fused_computation.23 | loop fusion | flops 11534336 | bytes 12607504 | tf_op jit(solution)/shard_map/add | solution.py:41
  (167 shorter events, 66.7 us)
Async XLA Ops:
  0.6 9.5 %collective-permute-start.1 = (f32[1,1,8,2,256]{4,3,2,1,0:T(2,128)}, f32[1,1,8,2,256]{4,3,2,1,0:T(2,128)S(1)}, u32[]{:S(2)}, u32[]{:S(2)}) collective-permute-start(f32[1,1,8,2,256]{4,3,2,1,0:T(2,128)} %bitcast.209), channel_id=1, source_target_pairs={{16,0},{32,16},{48,32},{64,48},{80,64},{96,80},{112,96},{17,1},{33... | collective-permute-start | bytes 49160 | tf_op jit(solution)/shard_map/ppermute | solution.py:26
  2.6 7.6 %collective-permute-start = (f32[1,1,8,2,256]{4,3,2,1,0:T(2,128)}, f32[1,1,8,2,256]{4,3,2,1,0:T(2,128)S(1)}, u32[]{:S(2)}, u32[]{:S(2)}) collective-permute-start(f32[1,1,8,2,256]{4,3,2,1,0:T(2,128)} %bitcast.210), channel_id=1, source_target_pairs={{0,16},{16,32},{32,48},{48,64},{64,80},{80,96},{96,112},{1,17},{17... | collective-permute-start | bytes 49160 | tf_op jit(solution)/shard_map/ppermute | solution.py:25
  6.0 4.2 copy-start.4
  10.2 6.4 collective-permute-start.3
  14.6 8.5 %collective-permute-start.2 = (f32[3,1,8,2,256]{4,3,2,1,0:T(2,128)S(1)}, f32[3,1,8,2,256]{4,3,2,1,0:T(2,128)S(1)}, u32[]{:S(2)}, u32[]{:S(2)}) collective-permute-start(f32[3,1,8,2,256]{4,3,2,1,0:T(2,128)S(1)} %pad_maximum_fusion.19), channel_id=1, source_target_pairs={{0,1},{1,2},{2,3},{3,4},{4,5},{5,6},{6,7},{7,8},{8,9},{9,10},{10,1... | collective-permute-start | bytes 147464 | tf_op jit(solution)/shard_map/ppermute | solution.py:25
  23.8 24.6 %copy-start.6 = (f32[8,256]{1,0:T(8,128)S(1)}, f32[8,256]{1,0:T(8,128)}, u32[]{:S(2)}) copy-start(f32[8,256]{1,0:T(8,128)} %param.9) | copy-start | bytes 24580
  31.7 8.1 %collective-permute-start.5 = (f32[3,8,2,256]{3,2,1,0:T(2,128)S(1)}, f32[3,8,2,256]{3,2,1,0:T(2,128)S(1)}, u32[]{:S(2)}, u32[]{:S(2)}) collective-permute-start(f32[3,8,2,256]{3,2,1,0:T(2,128)S(1)} %bitcast.247), channel_id=1, source_target_pairs={{0,1},{1,2},{2,3},{3,4},{4,5},{5,6},{6,7},{7,8},{8,9},{9,10},{10,1... | collective-permute-start | bytes 147464 | tf_op jit(solution)/shard_map/ppermute | solution.py:15
  33.6 7.8 %collective-permute-start.4 = (f32[3,8,2,256]{3,2,1,0:T(2,128)S(1)}, f32[3,8,2,256]{3,2,1,0:T(2,128)S(1)}, u32[]{:S(2)}, u32[]{:S(2)}) collective-permute-start(f32[3,8,2,256]{3,2,1,0:T(2,128)S(1)} %bitcast.244), channel_id=1, source_target_pairs={{1,0},{2,1},{3,2},{4,3},{5,4},{6,5},{7,6},{8,7},{9,8},{10,9},{11,1... | collective-permute-start | bytes 147464 | tf_op jit(solution)/shard_map/ppermute | solution.py:15
  41.5 4.4 collective-permute-start.6
  43.4 5.1 collective-permute-start.7
  186.9 5.4 collective-permute-start.9
  190.4 5.1 collective-permute-start.8
  195.5 6.1 collective-permute-start.11
  199.7 8.1 %collective-permute-start.10 = (f32[3,1,8,2,256]{4,3,2,1,0:T(2,128)S(1)}, f32[3,1,8,2,256]{4,3,2,1,0:T(2,128)S(1)}, u32[]{:S(2)}, u32[]{:S(2)}) collective-permute-start(f32[3,1,8,2,256]{4,3,2,1,0:T(2,128)S(1)} %pad_maximum_fusion.20), channel_id=1, source_target_pairs={{0,1},{1,2},{2,3},{3,4},{4,5},{5,6},{6,7},{7,8},{8,9},{9,10},{10,1... | collective-permute-start | bytes 147464 | tf_op jit(solution)/shard_map/ppermute | solution.py:25
  208.5 15.8 %copy-start.5 = (s32[2048,1]{0,1:T(1,128)S(1)}, s32[2048,1]{0,1:T(1,128)}, u32[]{:S(2)}) copy-start(s32[2048,1]{0,1:T(1,128)} %param.12) | copy-start | bytes 24580
  216.4 8.1 %collective-permute-start.13 = (f32[3,8,2,256]{3,2,1,0:T(2,128)S(1)}, f32[3,8,2,256]{3,2,1,0:T(2,128)S(1)}, u32[]{:S(2)}, u32[]{:S(2)}) collective-permute-start(f32[3,8,2,256]{3,2,1,0:T(2,128)S(1)} %bitcast.246), channel_id=1, source_target_pairs={{0,1},{1,2},{2,3},{3,4},{4,5},{5,6},{6,7},{7,8},{8,9},{9,10},{10,1... | collective-permute-start | bytes 147464 | tf_op jit(solution)/shard_map/ppermute | solution.py:15
  218.3 7.8 %collective-permute-start.12 = (f32[3,8,2,256]{3,2,1,0:T(2,128)S(1)}, f32[3,8,2,256]{3,2,1,0:T(2,128)S(1)}, u32[]{:S(2)}, u32[]{:S(2)}) collective-permute-start(f32[3,8,2,256]{3,2,1,0:T(2,128)S(1)} %bitcast.243), channel_id=1, source_target_pairs={{1,0},{2,1},{3,2},{4,3},{5,4},{6,5},{7,6},{8,7},{9,8},{10,9},{11,1... | collective-permute-start | bytes 147464 | tf_op jit(solution)/shard_map/ppermute | solution.py:15
  226.2 4.7 collective-permute-start.14
  228.1 5.1 collective-permute-start.15
  369.3 5.8 collective-permute-start.17
  373.1 5.1 collective-permute-start.16
  378.2 6.9 collective-permute-start.19
  382.7 8.1 %collective-permute-start.18 = (f32[3,1,8,2,256]{4,3,2,1,0:T(2,128)S(1)}, f32[3,1,8,2,256]{4,3,2,1,0:T(2,128)S(1)}, u32[]{:S(2)}, u32[]{:S(2)}) collective-permute-start(f32[3,1,8,2,256]{4,3,2,1,0:T(2,128)S(1)} %pad_maximum_fusion.21), channel_id=1, source_target_pairs={{0,1},{1,2},{2,3},{3,4},{4,5},{5,6},{6,7},{7,8},{8,9},{9,10},{10,1... | collective-permute-start | bytes 147464 | tf_op jit(solution)/shard_map/ppermute | solution.py:25
  399.4 8.6 %collective-permute-start.21 = (f32[3,8,2,256]{3,2,1,0:T(2,128)S(1)}, f32[3,8,2,256]{3,2,1,0:T(2,128)S(1)}, u32[]{:S(2)}, u32[]{:S(2)}) collective-permute-start(f32[3,8,2,256]{3,2,1,0:T(2,128)S(1)} %bitcast.245), channel_id=1, source_target_pairs={{0,1},{1,2},{2,3},{3,4},{4,5},{5,6},{6,7},{7,8},{8,9},{9,10},{10,1... | collective-permute-start | bytes 147464 | tf_op jit(solution)/shard_map/ppermute | solution.py:15
  401.3 7.8 %collective-permute-start.20 = (f32[3,8,2,256]{3,2,1,0:T(2,128)S(1)}, f32[3,8,2,256]{3,2,1,0:T(2,128)S(1)}, u32[]{:S(2)}, u32[]{:S(2)}) collective-permute-start(f32[3,8,2,256]{3,2,1,0:T(2,128)S(1)} %bitcast.242), channel_id=1, source_target_pairs={{1,0},{2,1},{3,2},{4,3},{5,4},{6,5},{7,6},{8,7},{9,8},{10,9},{11,1... | collective-permute-start | bytes 147464 | tf_op jit(solution)/shard_map/ppermute | solution.py:15
  409.2 4.4 collective-permute-start.22
  411.1 5.1 collective-permute-start.23
  413.5 75.7 %copy-start.8 = (s32[2048]{0:T(1024)S(1)}, s32[2048]{0:T(1024)}, u32[]{:S(2)}) copy-start(s32[2048]{0:T(1024)} %param.13) | copy-start | bytes 24580
  413.5 75.7 %copy-start.9 = (s32[2048]{0:T(1024)S(1)}, s32[2048]{0:T(1024)}, u32[]{:S(2)}) copy-start(s32[2048]{0:T(1024)} %param.14) | copy-start | bytes 24580
  489.1 45.7 %copy-start.7 = (f32[8,2,256]{2,1,0:T(2,128)}, f32[8,2,256]{2,1,0:T(2,128)S(1)}, u32[]{:S(2)}) copy-start(f32[8,2,256]{2,1,0:T(2,128)S(1)} %multiply_add_fusion) | copy-start | bytes 49156
  497.2 15.1 %all-to-all-start = ((f32[2,128,32]{2,0,1:T(2,128)}), f32[2,128,32]{2,0,1:T(2,128)S(1)}, u32[]{:S(2)}, u32[]{:S(2)}) async-start(f32[2,128,32]{2,0,1:T(2,128)} %copy.57), calls=%async_computation | async-start | bytes 262144 | tf_op jit(solution)/shard_map/all_to_all | solution.py:125
  534.9 2.0 copy-start.3
  536.9 4.4 collective-permute-start.24
  539.4 4.9 collective-permute-start.25
  560.0 6.2 collective-permute-start.26
  564.2 7.7 %collective-permute-start.27 = (f32[2050,1]{0,1:T(1,128)S(1)}, f32[2050,1]{0,1:T(1,128)S(1)}, u32[]{:S(2)}, u32[]{:S(2)}) collective-permute-start(f32[2050,1]{0,1:T(1,128)S(1)} %copy.60), channel_id=1, source_target_pairs={{0,1},{1,2},{2,3},{3,4},{4,5},{5,6},{6,7},{7,8},{8,9},{9,10},{10,1... | collective-permute-start | bytes 24608 | tf_op jit(solution)/shard_map/ppermute | solution.py:25
  585.1 2.0 copy-start
  587.1 4.3 collective-permute-start.28
  589.0 4.9 collective-permute-start.29
  609.7 6.2 collective-permute-start.30
  611.9 7.7 %collective-permute-start.31 = (f32[2050,1]{0,1:T(1,128)S(1)}, f32[2050,1]{0,1:T(1,128)S(1)}, u32[]{:S(2)}, u32[]{:S(2)}) collective-permute-start(f32[2050,1]{0,1:T(1,128)S(1)} %copy.64), channel_id=1, source_target_pairs={{0,1},{1,2},{2,3},{3,4},{4,5},{5,6},{6,7},{7,8},{8,9},{9,10},{10,1... | collective-permute-start | bytes 24608 | tf_op jit(solution)/shard_map/ppermute | solution.py:25
  632.5 2.0 copy-start.1
  634.5 4.3 collective-permute-start.32
  636.4 4.9 collective-permute-start.33
  657.0 6.2 collective-permute-start.34
  659.3 7.7 %collective-permute-start.35 = (f32[2050,1]{0,1:T(1,128)S(1)}, f32[2050,1]{0,1:T(1,128)S(1)}, u32[]{:S(2)}, u32[]{:S(2)}) collective-permute-start(f32[2050,1]{0,1:T(1,128)S(1)} %copy.68), channel_id=1, source_target_pairs={{0,1},{1,2},{2,3},{3,4},{4,5},{5,6},{6,7},{7,8},{8,9},{9,10},{10,1... | collective-permute-start | bytes 24608 | tf_op jit(solution)/shard_map/ppermute | solution.py:25
  679.8 2.0 copy-start.2
  681.8 4.3 collective-permute-start.36
  683.7 4.9 collective-permute-start.37
  704.4 6.4 collective-permute-start.38
  706.8 7.7 %collective-permute-start.39 = (f32[2050,1]{0,1:T(1,128)S(1)}, f32[2050,1]{0,1:T(1,128)S(1)}, u32[]{:S(2)}, u32[]{:S(2)}) collective-permute-start(f32[2050,1]{0,1:T(1,128)S(1)} %copy.72), channel_id=1, source_target_pairs={{0,1},{1,2},{2,3},{3,4},{4,5},{5,6},{6,7},{7,8},{8,9},{9,10},{10,1... | collective-permute-start | bytes 24608 | tf_op jit(solution)/shard_map/ppermute | solution.py:25
